TPU v7x, 32 devices: a whole 2x2x4 slice. The times are simulated.
32 devices in a mesh: member: 2 (over x), wave: 8 (over z, y), lev: 2 (over core).
Axes of the slice: x: 2, y: 2, z: 4, core: 2. Of those that a mesh axis runs over, the one named last changes fastest.
Arguments:
- grid: bfloat16 [128, 320, 2, 1280], P(('member', 'lev'), 'wave'), parts along dimension 0, may hold values from -6 to 6
- lat_order: int32 [320], replicated, may hold values from 0 to 319, each once
- wave_order: int32 [640], replicated, may hold values from 0 to 639, as said below
- trim: int32 [640], replicated, may hold values from 0 to 4, as said below
- legendre: bfloat16 [640, 640, 320], P('wave'), may hold values from -0.3125 to 0.3125
- modes_in: bfloat16 [64, 64], replicated, may hold values from -0.75 to 0.75
- modes_out: bfloat16 [64, 64], replicated, may hold values from -0.75 to 0.75
- implicit: float32 [64], replicated, may hold values from 0.3 to 30
Outputs:
- fourier_out: bfloat16 [128, 320, 2, 1280], P(('member', 'lev'), 'wave'), parts along dimension 0
There are 2 independent parts, one for each index of `member`. A program takes and returns all parts, laid end to end along the dimension named above; an argument that names none is the same for every part. Nothing has to cross between parts.
Inputs may be any that keep to these rules, and one draw needn't show every extreme that they name: `wave_order`: a permutation of 0 to 639 in which entries 2i and 2i+1 are k and 639-k for some k. `trim`: for wavenumber m, how many blocks of 64 latitudes nearest each pole take no part in its products.
All inputs are finite; a program needn't handle non-finite values.
Results may differ from a plain program's by a relative error of at most 0.015.
Values may be sent and summed in bfloat16 or wider, within the bound.
A program may use at most 192 MiB of HBM per device.

v0:
```python
import math

import jax
import jax.numpy as jnp
from jax import lax
from jax.sharding import PartitionSpec as P

LBLK = 64


def fourier_table(wave_order, lon_count):
    longitude = jnp.arange(lon_count, dtype=jnp.int32)
    phase_int = longitude[:, None] * wave_order[None, :] % lon_count
    angles = phase_int.astype(jnp.float32) * (2.0 * math.pi / lon_count)
    dft_table = jnp.stack([jnp.cos(angles), -jnp.sin(angles)], 2) * (1.0 / math.sqrt(lon_count))
    return dft_table.reshape(lon_count, 2 * wave_order.shape[0])


def keep_masks(wavenum, trim, row_count, lat_count):
    row_index = jnp.arange(row_count, dtype=jnp.int32)
    latitude = jnp.arange(lat_count, dtype=jnp.int32)
    row_keep = wavenum[:, None] + row_index[None, :] < row_count
    lat_keep = latitude[None, :] >= LBLK * trim[wavenum][:, None]
    return (row_keep, lat_keep)


def forward(received, legendre_part, row_keep, lat_keep, fields):
    wave_count, row_count, lat_count = legendre_part.shape
    columns_in = received.reshape(fields, lat_count, 2, wave_count, 2).transpose(3, 2, 1, 4, 0)
    columns_in = columns_in.reshape(wave_count, 2, lat_count, 2 * fields)
    columns_in = jnp.where(lat_keep[:, None, :, None], columns_in, jnp.zeros((), jnp.bfloat16))
    paired = legendre_part.reshape(wave_count, row_count // 2, 2, lat_count)
    coeffs = jnp.einsum("wael,welx->waex", paired, columns_in, preferred_element_type=jnp.float32)
    rows_ok = row_keep.reshape(wave_count, row_count // 2, 2)[..., None]
    coeffs = jnp.where(rows_ok, coeffs, jnp.float32(0.0))
    return coeffs.astype(jnp.bfloat16).reshape(wave_count, row_count // 2, 2, 2, fields)


def vertical(coeffs, wavenum, modes_in, modes_out, implicit):
    wave_count = coeffs.shape[0]
    row_count = coeffs.shape[1] * 2
    degree = (wavenum[:, None] + jnp.arange(row_count, dtype=jnp.int32)[None, :]).astype(
        jnp.float32
    )
    factor = (degree * (degree + 1.0) / float(row_count * (row_count - 1))).reshape(
        wave_count, row_count // 2, 2
    )
    modal_part = jnp.einsum("waecl,kl->waeck", coeffs, modes_in, preferred_element_type=jnp.float32)
    scaled = (modal_part / (1.0 + factor[..., None, None] * implicit)).astype(jnp.bfloat16)
    solved = jnp.einsum("waeck,lk->waecl", scaled, modes_out, preferred_element_type=jnp.float32)
    return solved.astype(jnp.bfloat16)


def inverse(solved, legendre_part, lat_keep, fields):
    wave_count, half_rows = (solved.shape[0], solved.shape[1])
    lat_count = legendre_part.shape[2]
    paired = legendre_part.reshape(wave_count, half_rows, 2, lat_count)
    flattened = solved.reshape(wave_count, half_rows, 2, 2 * fields)
    parity_sums = jnp.einsum(
        "wael,waex->welx", paired, flattened, preferred_element_type=jnp.float32
    )
    parity_sums = jnp.where(lat_keep[:, None, :, None], parity_sums, jnp.float32(0.0))
    north_side = parity_sums[:, 0] + parity_sums[:, 1]
    south_side = parity_sums[:, 0] - parity_sums[:, 1]
    hemispheres = jnp.stack([north_side, south_side], 2).astype(jnp.bfloat16)
    hemispheres = hemispheres.reshape(wave_count, lat_count, 2, 2, fields).transpose(4, 1, 2, 0, 3)
    return hemispheres.reshape(fields, lat_count, 2, 2 * wave_count)


def local(grid, lat_order, wave_order, trim, legendre, modes_in, modes_out, implicit):
    half_fields, lat_pairs, lon_count = (grid.shape[0], grid.shape[1], grid.shape[3])
    per_device = legendre.shape[0]
    row_count, lat_count = (legendre.shape[1], legendre.shape[2])
    inverse_order = (
        jnp.zeros((lat_count,), jnp.int32).at[lat_order].set(jnp.arange(lat_count, dtype=jnp.int32))
    )
    dft_table = fourier_table(wave_order, lon_count)
    upper_part = dft_table.astype(jnp.bfloat16)
    lower_part = (dft_table - upper_part.astype(jnp.float32)).astype(jnp.bfloat16)
    grid_rows = grid.reshape(-1, lon_count)
    spectra = jnp.dot(grid_rows, upper_part, preferred_element_type=jnp.float32)
    spectra = (spectra + jnp.dot(grid_rows, lower_part, preferred_element_type=jnp.float32)).astype(
        jnp.bfloat16
    )
    spectra = (
        lax.optimization_barrier(spectra).astype(jnp.float32).reshape(half_fields, lat_pairs, 2, -1)
    )
    symmetric = jnp.stack(
        [spectra[:, :, 0] + spectra[:, :, 1], spectra[:, :, 0] - spectra[:, :, 1]], 2
    ).astype(jnp.bfloat16)
    first_slot = lax.axis_index("wave") * per_device
    my_waves = lax.dynamic_slice_in_dim(wave_order, first_slot, per_device)
    levels = lax.axis_size("lev")
    lev_share = per_device // levels
    offset = lax.axis_index("lev") * lev_share
    row_keep, lat_keep = keep_masks(my_waves, trim, row_count, lat_count)
    received = lax.all_to_all(symmetric, "wave", split_axis=3, concat_axis=1, tiled=True)
    received = jnp.take(received, inverse_order, axis=1)
    coeffs = forward(received, legendre, row_keep, lat_keep, half_fields)
    gathered = lax.all_to_all(coeffs, "lev", split_axis=0, concat_axis=4, tiled=True)
    wavenum = lax.dynamic_slice_in_dim(my_waves, offset, lev_share)
    solved = vertical(gathered, wavenum, modes_in, modes_out, implicit)
    returned = lax.all_to_all(solved, "lev", split_axis=4, concat_axis=0, tiled=True)
    result = inverse(returned, legendre, lat_keep, half_fields)
    result = jnp.take(result, lat_order, axis=1)
    fourier_out = lax.all_to_all(result, "wave", split_axis=1, concat_axis=3, tiled=True)
    return fourier_out


def solution(mesh):
    in_specs = (
        P(("member", "lev"), "wave", None, None),
        P(),
        P(),
        P(),
        P("wave", None, None),
        P(),
        P(),
        P(),
    )
    out_specs = P(("member", "lev"), "wave", None, None)
    return jax.shard_map(local, mesh=mesh, in_specs=in_specs, out_specs=out_specs, check_vma=False)
```

profile of v0, /device:TPU:15, one launch (start us, length us, event | category | flops | bytes accessed | tf_op | source)
XLA Modules:
  0.0 909.9 jit_solution(9252496254895439674)
XLA Ops:
  0.0 0.0 copy-start
  0.0 14.0 %fusion.18 = (f32[1280,640,1]{1,0,2:T(8,128)S(1)}, f32[1280,640,1]{1,0,2:T(8,128)S(1)}) fusion(s32[640]{0:T(1024)} %param.12), kind=kLoop, calls=%fused_computation.38 | loop fusion | flops 8192000 | bytes 6556160 | tf_op jit(solution)/shard_map/cos | solution.py:15
  14.0 2.2 subtract_convert_fusion.2
  16.3 10.5 %copy.68 = bf16[1280,640,2]{0,2,1:T(2,128)(2,1)} copy(bf16[1280,640,2]{1,0,2:T(8,128)(2,1)} %get-tuple-element.13) | data formatting | bytes 6553600 | tf_op jit(solution)/shard_map/convert_element_type | solution.py:78
  26.8 7.7 convert_element_type.83
  34.5 14.2 %reshape.250 = bf16[2560,1280]{1,0:T(8,128)(2,1)} reshape(bf16[32,40,2,1280]{3,2,1,0:T(2,128)(2,1)} %param.10) | data formatting | bytes 13107200 | tf_op jit(solution)/shard_map/reshape | solution.py:80
  48.6 7.5 copy.69
  56.2 0.0 slice-start
  56.2 7.8 convert_element_type.86
  64.0 0.0 slice-start.1
  64.0 15.1 %fusion.27 = f32[1280,2560]{1,0:T(8,128)} fusion(bf16[1280,1280]{0,1:T(8,128)(2,1)} %convert_element_type.83, bf16[2560,1280]{1,0:T(8,128)(2,1)} %reshape.250), kind=kOutput, calls=%fused_computation.59 | convolution fusion | flops 8388608000 | bytes 22937600 | tf_op jit(solution)/shard_map/dot_general | solution.py:81
  79.1 0.0 slice-done
  79.1 0.0 slice-done.1
  79.1 14.5 %fusion.6 = bf16[2560,1280]{0,1:T(8,128)(2,1)} fusion(f32[1280,2560]{1,0:T(8,128)} %fusion.27, bf16[1280,1280]{0,1:T(8,128)(2,1)} %convert_element_type.86, bf16[2560,1280]{1,0:T(8,128)(2,1)S(1)} %bitcast.80), kind=kOutput, calls=%fused_computation.16 | convolution fusion | flops 8395161600 | bytes 29491200 | tf_op jit(solution)/shard_map/dot_general | solution.py:82
  93.6 10.6 %copy.70 = f32[2560,1280]{1,0:T(8,128)} copy(bf16[2560,1280]{0,1:T(8,128)(2,1)} %fusion.6) | data formatting | bytes 19660800 | tf_op jit(solution)/shard_map/reshape | solution.py:86
  104.2 15.7 %reshape.260 = f32[32,40,2,1280]{3,2,1,0:T(2,128)} reshape(f32[2560,1280]{1,0:T(8,128)} %copy.70) | data formatting | bytes 26214400 | tf_op jit(solution)/shard_map/reshape | solution.py:86
  119.9 17.0 %add_convert_fusion.1 = (bf16[32,40,1,1280]{3,2,1,0:T(2,128)(2,1)S(1)}, bf16[32,40,1,1280]{3,2,1,0:T(2,128)(2,1)S(1)}) fusion(f32[32,40,2,1280]{3,2,1,0:T(2,128)} %reshape.260), kind=kLoop, calls=%fused_computation.27 | loop fusion | flops 6553600 | bytes 19660800 | tf_op jit(solution)/shard_map/convert.5
  136.9 16.0 %pad_maximum_fusion.1 = bf16[32,40,2,1280]{3,2,1,0:T(2,128)(2,1)} fusion(bf16[32,40,1,1280]{3,2,1,0:T(2,128)(2,1)S(1)} %get-tuple-element.11, bf16[32,40,1,1280]{3,2,1,0:T(2,128)(2,1)S(1)} %get-tuple-element.10), kind=kLoop, calls=%fused_computation.25 | loop fusion | flops 13107200 | bytes 13107200 | tf_op jit(solution)/shard_map/stack | solution.py:88
  152.8 32.9 %copy.71 = bf16[32,40,2,1280]{1,0,2,3:T(8,128)(2,1)} copy(bf16[32,40,2,1280]{3,2,1,0:T(2,128)(2,1)} %pad_maximum_fusion.1) | data formatting | bytes 13107200 | tf_op jit(solution)/shard_map/stack | solution.py:88
  185.7 34.8 %reshape.306 = bf16[8,2,204800]{2,1,0:T(2,128)(2,1)} reshape(bf16[1280,2,32,40]{3,2,1,0:T(8,128)(2,1)} %bitcast.66) | data formatting | bytes 13107200
  220.5 5.7 all-to-all-start
  226.2 0.0 copy-start.2
  226.2 0.0 copy-start.1
  226.2 0.0 copy-start.3
  226.2 48.0 %copy.76 = bf16[80,640,320]{2,0,1:T(8,128)(2,1)} copy(bf16[80,640,320]{1,2,0:T(8,128)(2,1)} %param.14) | data formatting | bytes 65536000 | tf_op args[4]
  274.2 0.8 dynamic_slice.10
  275.0 0.1 fusion.20
  275.1 0.1 copy.79
  275.1 0.0 copy-done.2
  275.2 2.9 scatter_custom_fusion
  278.1 0.8 compare_select_fusion.2
  278.9 0.0 copy-done.1
  278.9 1.4 gather_fusion
  280.4 0.1 iota_compare_fusion
  280.5 0.2 add_compare_fusion
  280.7 0.0 copy-done.3
  280.7 4.2 multiply_add_fusion
  285.0 82.5 %all-to-all-done = bf16[8,2,204800]{2,1,0:T(2,128)(2,1)} async-done(((bf16[8,2,204800]{2,1,0:T(2,128)(2,1)}), bf16[8,2,204800]{2,1,0:T(2,128)(2,1)}, u32[]{:S(2)}, u32[]{:S(2)}) %all-to-all-start) | async-done | bytes 6553632 | tf_op jit(solution)/shard_map/all_to_all | solution.py:97
  367.4 36.1 %reshape.307 = bf16[1280,2,32,40]{3,2,1,0:T(8,128)(2,1)} reshape(bf16[8,2,204800]{2,1,0:T(2,128)(2,1)} %all-to-all-done) | data formatting | bytes 13107200
  403.5 29.9 %copy.89 = bf16[32,40,2,8,160]{4,0,2,1,3:T(8,128)(2,1)} copy(bf16[32,40,2,8,160]{1,0,2,4,3:T(8,128)(2,1)} %bitcast.67) | data formatting | bytes 13107200 | tf_op jit(solution)/shard_map/all_to_all | solution.py:97
  433.4 14.6 %gather_fusion.1 = bf16[320,32,2,160]{3,1,2,0:T(8,128)(2,1)} fusion(bf16[32,320,2,160]{3,0,2,1:T(8,128)(2,1)} %bitcast.69, s32[1024]{0:T(1024)S(1)} %pad_clamp_fusion.1), kind=kCustom, calls=%fused_computation.clone | custom fusion | bytes 13108480 | tf_op jit(solution)/shard_map/jit(_take)/gather | solution.py:98
  448.0 10.3 %select_bitcast_fusion.2 = bf16[32,320,2,160]{3,0,2,1:T(8,128)(2,1)} fusion(bf16[320,32,2,160]{3,1,2,0:T(8,128)(2,1)} %gather_fusion.1, pred[320]{0:T(512)(128)(4,1)S(1)} %compare_and_fusion.1), kind=kLoop, calls=%fused_computation.15 | loop fusion | flops 3276800 | bytes 13107520 | tf_op jit(solution)/shard_map/jit(_take)/select_n | solution.py:98
  458.3 17.0 %copy.74 = bf16[32,320,2,160]{1,0,3,2:T(8,128)(2,1)} copy(bf16[32,320,2,160]{3,0,2,1:T(8,128)(2,1)} %select_bitcast_fusion.2) | data formatting | bytes 13107200 | tf_op jit(solution)/shard_map/jit(_take)/select_n | solution.py:98
  475.4 28.6 %fusion.4 = bf16[80,320,2,64]{1,3,2,0:T(8,128)(2,1)} fusion(bf16[80,320,2,320]{3,0,2,1:T(8,128)(2,1)} %bitcast.64, bf16[80,2,320,64]{2,3,0,1:T(8,128)(2,1)} %bitcast.76, pred[80,320]{1,0:T(8,128)(4,1)S(1)} %iota_compare_fusion, pred[80,320,2]{1,2,0:T(4,128)(4,1)S(1)} %add_compare_fusion), kind=kOutput, calls=%fused_computation.9 | convolution fusion | flops 2106982400 | bytes 45952000 | tf_op jit(solution)/shard_map/wael,welx->waex/dot_general | solution.py:33
  504.0 11.8 %all_to_all.69 = bf16[80,320,2,2,32]{1,4,3,2,0:T(8,128)(2,1)S(1)} all-to-all(bf16[80,320,2,2,32]{1,4,3,2,0:T(8,128)(2,1)} %bitcast.77), channel_id=1, replica_groups=mesh['member'=2,'wave'=8,'lev'=2] {'lev'}, dimensions={0} | all-to-all | bytes 13107200 | tf_op jit(solution)/shard_map/all_to_all | solution.py:100
  515.7 0.0 copy-start.4
  515.7 4.4 copy.78
  520.2 0.0 copy-done
  520.2 0.0 copy-done.4
  520.2 9.7 %convolution_convert_fusion = bf16[40,320,2,2,64]{1,4,3,2,0:T(8,128)(2,1)} fusion(bf16[40,320,2,2,64]{1,4,3,2,0:T(8,128)(2,1)} %bitcast.78, f32[40,320,2,64]{1,3,2,0:T(8,128)} %multiply_add_fusion, bf16[64,64]{1,0:T(8,128)(2,1)S(1)} %copy-done, bf16[64,64]{1,0:T(8,128)(2,1)S(1)} %copy-done.4), kind=kOutput, calls=%fused_computation.23 | convolution fusion | flops 848691200 | bytes 19677184 | tf_op jit(solution)/shard_map/waeck,lk->waecl/dot_general | solution.py:50
  529.9 13.6 %copy.80 = bf16[40,320,2,2,64]{1,3,2,0,4:T(2,128)(2,1)S(1)} copy(bf16[40,320,2,2,64]{1,4,3,2,0:T(8,128)(2,1)} %convolution_convert_fusion) | data formatting | bytes 13107200 | tf_op jit(solution)/shard_map/convert_element_type | solution.py:51
  543.5 11.6 %all_to_all.70 = bf16[40,320,2,2,64]{1,3,2,0,4:T(2,128)(2,1)} all-to-all(bf16[40,320,2,2,64]{1,3,2,0,4:T(2,128)(2,1)S(1)} %copy.80), channel_id=1, replica_groups=mesh['member'=2,'wave'=8,'lev'=2] {'lev'}, dimensions={4} | all-to-all | bytes 13107200 | tf_op jit(solution)/shard_map/all_to_all | solution.py:103
  555.1 8.0 copy.81
  563.0 29.8 %select_bitcast_fusion = f32[80,2,320,64]{2,3,1,0:T(8,128)} fusion(bf16[80,320,2,64]{1,3,2,0:T(8,128)(2,1)S(1)} %bitcast.70, bf16[80,320,2,320]{3,0,2,1:T(8,128)(2,1)} %bitcast.65, pred[80,320]{1,0:T(8,128)(4,1)S(1)} %iota_compare_fusion), kind=kOutput, calls=%fused_computation.10 | convolution fusion | flops 2100428800 | bytes 52454400 | tf_op jit(solution)/shard_map/wael,waex->welx/dot_general | solution.py:59
  592.8 7.0 add_convert_fusion
  599.8 4.7 pad_maximum_fusion
  604.5 17.3 %copy.83 = bf16[32,320,2,160]{3,0,2,1:T(8,128)(2,1)} copy(bf16[32,320,2,160]{1,0,3,2:T(8,128)(2,1)} %bitcast.71) | data formatting | bytes 13107200 | tf_op jit(solution)/shard_map/reshape | solution.py:67
  621.8 14.6 %gather_fusion.2 = bf16[320,32,2,160]{3,1,2,0:T(8,128)(2,1)} fusion(bf16[32,320,2,160]{3,0,2,1:T(8,128)(2,1)} %copy.83, s32[1024]{0:T(1024)S(1)} %pad_clamp_fusion), kind=kCustom, calls=%fused_computation.1.clone | custom fusion | bytes 13108480 | tf_op jit(solution)/shard_map/jit(_take)/gather | solution.py:105
  636.4 6.0 select_bitcast_fusion.1
  642.5 231.8 %all_to_all.71 = bf16[32,320,2,160]{3,0,2,1:T(8,128)(2,1)} all-to-all(bf16[32,320,2,160]{3,0,2,1:T(8,128)(2,1)S(1)} %select_bitcast_fusion.1), channel_id=1, replica_groups=mesh['member'=2,'wave'=8,'lev'=2] {'wave'}, dimensions={1} | all-to-all | bytes 13107200 | tf_op jit(solution)/shard_map/all_to_all | solution.py:106
  874.2 13.8 %copy.91 = bf16[32,40,2,8,160]{4,3,2,1,0:T(8,128)(2,1)} copy(bf16[32,40,2,8,160]{4,0,2,1,3:T(8,128)(2,1)} %bitcast.68) | data formatting | bytes 13107200 | tf_op jit(solution)/shard_map/all_to_all | solution.py:106
  888.0 21.4 %reshape.303 = bf16[32,40,2,1280]{3,2,1,0:T(2,128)(2,1)} reshape(bf16[32,40,2,8,160]{4,3,2,1,0:T(8,128)(2,1)} %copy.91) | data formatting | bytes 13107200 | tf_op jit(solution)/shard_map/all_to_all | solution.py:106
  (11 shorter events, 0.1 us)
Async XLA Ops:
  0.0 520.2 %copy-start = (bf16[64,64]{1,0:T(8,128)(2,1)S(1)}, bf16[64,64]{1,0:T(8,128)(2,1)}, u32[]{:S(2)}) copy-start(bf16[64,64]{1,0:T(8,128)(2,1)} %param.16) | copy-start | bytes 24580
  56.2 23.0 %slice-start = ((s8[6553600]{0:T(1024)(128)(4,1)}), s8[2359296]{0:T(1024)(128)(4,1)S(1)}, s32[]{:S(2)}) async-start(s8[6553600]{0:T(1024)(128)(4,1)} %bitcast.79), calls=%async_computation.4 | async-start | bytes 4718592
  64.0 15.1 %slice-start.1 = ((s8[6553600]{0:T(1024)(128)(4,1)}), s8[4194304]{0:T(1024)(128)(4,1)S(1)}, s32[]{:S(2)}) async-start(s8[6553600]{0:T(1024)(128)(4,1)} %bitcast.79), calls=%async_computation.5 | async-start | bytes 8388608
  220.5 146.9 %all-to-all-start = ((bf16[8,2,204800]{2,1,0:T(2,128)(2,1)}), bf16[8,2,204800]{2,1,0:T(2,128)(2,1)}, u32[]{:S(2)}, u32[]{:S(2)}) async-start(bf16[8,2,204800]{2,1,0:T(2,128)(2,1)} %reshape.306), calls=%async_computation | async-start | bytes 13107200 | tf_op jit(solution)/shard_map/all_to_all | solution.py:97
  226.2 48.9 %copy-start.2 = (s32[320]{0:T(512)S(1)}, s32[320]{0:T(512)}, u32[]{:S(2)}) copy-start(s32[320]{0:T(512)} %param.11) | copy-start | bytes 3844
  226.2 52.6 %copy-start.1 = (s32[640]{0:T(1024)S(1)}, s32[640]{0:T(1024)}, u32[]{:S(2)}) copy-start(s32[640]{0:T(1024)} %param.13) | copy-start | bytes 7684
  226.2 54.5 %copy-start.3 = (f32[64]{0:T(128)S(1)}, f32[64]{0:T(128)}, u32[]{:S(2)}) copy-start(f32[64]{0:T(128)} %param.17) | copy-start | bytes 772
  515.7 4.4 copy-start.4
where the time goes:
time: 928 us; the launch traced here: 910 us
  local copies, waits for them, and re-layouts  386 us (42%)
  blocking collectives  255 us (27%)
  matrix products  97.7 us (11%)
  other arithmetic  82.7 us (9%)
  waiting for transfers between devices  82.5 us (9%)
    all_to_all x1, blocking collectives, local(): lax.all_to_all(result, 'wave', split_axis=1, concat_axis=3, tiled=True)  232 us
    unnamed x17, local copies, waits for them, and re-layouts  119 us
    all_to_all x1, waiting for transfers between devices, local(): lax.all_to_all(symmetric, 'wave', split_axis=3, concat_axis=1, tiled=True)  82.5 us
    all_to_all x2, local copies, waits for them, and re-layouts, local(): lax.all_to_all(result, 'wave', split_axis=1, concat_axis=3, tiled=True)  35.2 us
    another operation x1, local copies, waits for them, and re-layouts, local(): jnp.stack([spectra[:, :, 0] + spectra[:, :, 1], spectra[:, :, 0] - spectr...  32.9 us
    all_to_all x1, local copies, waits for them, and re-layouts, local(): lax.all_to_all(symmetric, 'wave', split_axis=3, concat_axis=1, tiled=True)  29.9 us
    dot_general x1, matrix products, inverse(): jnp.einsum('wael,waex->welx', paired, flattened, preferred_element_type=j...  29.8 us
    dot_general x1, matrix products, forward(): jnp.einsum('wael,welx->waex', paired, columns_in, preferred_element_type=...  28.6 us
  transfers between devices with their start and end apart: 1, of which 1 were waited for; matrix products, arithmetic and copies ran while one was open for 6% of the time, Pallas kernels for 0%

commit v1 on v0

v1 whole, which is shorter than its diff:
```python
import functools
import math

import jax
import jax.numpy as jnp
from jax import lax
from jax.experimental import pallas as pl
from jax.experimental.pallas import tpu as pltpu
from jax.sharding import PartitionSpec as P

LBLK = 64
LANES = 128
F32 = jnp.float32
BF16 = jnp.bfloat16


def dft_kernel(slots, block, grid_ref, cos_a, sin_a, cos_b, sin_b, out_ref, table, held):
    step = pl.program_id(0)
    waves = cos_b.shape[0]
    fields = grid_ref.shape[0]
    width = 2 * fields

    @pl.when(step == 0)
    def _():
        for a in range(cos_a.shape[1]):
            ca, sa = cos_a[:, a : a + 1], sin_a[:, a : a + 1]
            cols = slice(a * LANES, (a + 1) * LANES)
            table[:waves, cols] = (ca * cos_b[...] - sa * sin_b[...]).astype(BF16)
            table[waves:, cols] = (-(sa * cos_b[...] + ca * sin_b[...])).astype(BF16)

    rows = jnp.concatenate(
        [grid_ref[:, s].reshape(width, grid_ref.shape[3]) for s in range(block)], 0
    )
    real = lax.dot_general(
        table[:waves], rows, (((1,), (1,)), ((), ())), preferred_element_type=F32
    )
    imag = lax.dot_general(
        table[waves:], rows, (((1,), (1,)), ((), ())), preferred_element_type=F32
    )
    for s in range(block):
        part = slice(s * width, (s + 1) * width)
        both = jnp.concatenate([real[:, part], imag[:, part]], 1)
        held[pl.ds(step * block + s, waves, stride=slots), :] = both

    @pl.when(step == pl.num_programs(0) - 1)
    def _():
        chunk = 16

        @pl.loop(0, waves // chunk)
        def _(i):
            piece = held[pl.ds(pl.multiple_of(i * chunk * slots, 8), chunk * slots), :]
            out_ref[pl.ds(i * chunk, chunk)] = piece.reshape(chunk, slots, 2 * width).astype(BF16)


def dft(grid, wave_order):
    fields, slots, _, lon_count = grid.shape
    waves = wave_order.shape[0]
    scale = 2.0 * math.pi / lon_count

    def angles(longitude):
        phase = wave_order[:, None] * longitude[None, :] % lon_count
        return phase.astype(F32) * scale

    part_a = angles(jnp.arange(lon_count // LANES, dtype=jnp.int32) * LANES)
    part_b = angles(jnp.arange(LANES, dtype=jnp.int32))
    norm = 1.0 / math.sqrt(lon_count)
    block = 4 if slots % 4 == 0 else (2 if slots % 2 == 0 else 1)
    whole = lambda x: pl.BlockSpec(x.shape, lambda i: (0, 0))
    tables = [jnp.cos(part_a) * norm, jnp.sin(part_a) * norm, jnp.cos(part_b), jnp.sin(part_b)]
    return pl.pallas_call(
        functools.partial(dft_kernel, slots, block),
        grid=(slots // block,),
        in_specs=[pl.BlockSpec((fields, block, 2, lon_count), lambda i: (0, i, 0, 0))]
        + [whole(x) for x in tables],
        out_specs=pl.BlockSpec((waves, slots, 4 * fields), lambda i: (0, 0, 0)),
        out_shape=jax.ShapeDtypeStruct((waves, slots, 4 * fields), BF16),
        scratch_shapes=[
            pltpu.VMEM((2 * waves, lon_count), BF16),
            pltpu.VMEM((waves * slots, 4 * fields), F32),
        ],
        compiler_params=pltpu.CompilerParams(vmem_limit_bytes=56 * 2**20),
    )(grid, *tables)


def spectral_kernel(
    rows_total, wave_ref, start_ref, block_ref, data_ref, legendre_ref, to_phys, to_slot, keep_code,
    mix_in, mix_out, implicit_ref, out_ref,
):
    i = pl.program_id(0)
    m = wave_ref[i]
    first = start_ref[i]
    owners, levels, _, slots, part = data_ref.shape
    lats = owners * slots
    width = levels * part
    mapped = [data_ref[:, v, 0].reshape(lats, part) for v in range(levels)]
    x = jnp.concatenate(mapped, 1)
    x = jnp.dot(to_phys[...], x, preferred_element_type=F32)
    lane = lax.broadcasted_iota(jnp.int32, (lats, width), 1)
    lat = lax.broadcasted_iota(jnp.int32, (lats, width), 0)
    north = lane % 2 == 0
    lat_ok = lat >= first
    sym = jnp.where(
        north, x + pltpu.roll(x, width - 1, 1), pltpu.roll(x, 1, 1) - x
    )
    sym = jnp.where(lat_ok, sym, 0.0).astype(BF16)
    basis = legendre_ref[0]
    y = jnp.dot(basis, sym, preferred_element_type=F32)
    y = jnp.where(keep_code[...] < rows_total - m, y, 0.0).astype(BF16)
    modal = jnp.dot(y, mix_in[...], preferred_element_type=F32)
    degree = (m + lax.broadcasted_iota(jnp.int32, (rows_total, 1), 0)).astype(F32)
    factor = degree * (degree + 1.0) / float(rows_total * (rows_total - 1))
    scaled = (modal / (1.0 + factor * implicit_ref[...])).astype(BF16)
    solved = jnp.dot(scaled, mix_out[...], preferred_element_type=F32).astype(BF16)
    o = lax.dot_general(basis, solved, (((0,), (0,)), ((), ())), preferred_element_type=F32)
    o = jnp.where(lat_ok, o, 0.0).astype(BF16)
    o = jnp.dot(to_slot[...], o, preferred_element_type=F32).astype(BF16)
    for v in range(levels):
        out_ref[:, v, 0] = o[:, v * part : (v + 1) * part].reshape(owners, slots, part)


def spectral(
    data, legendre, first_block, my_waves, my_starts, lat_order, modes_in, modes_out, implicit
):
    owners, levels, mine, slots, part = data.shape
    rows_total, lats = legendre.shape[1], legendre.shape[2]
    fields = part // 4
    width = levels * part
    order = jnp.arange(lats, dtype=jnp.int32)
    to_slot = (lat_order[:, None] == order[None, :]).astype(BF16)
    to_phys = to_slot.T
    lane = jnp.arange(width, dtype=jnp.int32)
    row = jnp.arange(rows_total, dtype=jnp.int32)
    keep_code = jnp.where(row[:, None] % 2 == lane[None, :] % 2, row[:, None], 2 * rows_total)
    modes = modes_in.shape[0]
    in_by_lane = modes_in.T.reshape(levels, fields, modes)
    sign = jnp.array([[1.0, 1.0], [1.0, -1.0]], F32)
    eye = jnp.eye(2, dtype=F32)
    mix_in = jnp.einsum("vfk,cd,hg->vcfhgdk", in_by_lane.astype(F32), eye, sign)
    mix_in = mix_in.reshape(width, 4 * modes).astype(BF16)
    out_by_lane = modes_out.reshape(levels, fields, modes)
    mix_out = jnp.einsum("vfk,cd,hg->gdkvcfh", out_by_lane.astype(F32), eye, eye)
    mix_out = mix_out.reshape(4 * modes, width).astype(BF16)
    implicit_lane = jnp.tile(implicit, 4)[None, :]
    block = pl.BlockSpec((owners, levels, 1, slots, part), lambda i, *_: (0, 0, i, 0, 0))
    whole = lambda x: pl.BlockSpec(x.shape, lambda i, *_: (0, 0))
    consts = [to_phys, to_slot, keep_code, mix_in, mix_out, implicit_lane]
    return pl.pallas_call(
        functools.partial(spectral_kernel, rows_total),
        grid_spec=pltpu.PrefetchScalarGridSpec(
            num_scalar_prefetch=3,
            grid=(mine,),
            in_specs=[
                block,
                pl.BlockSpec((1, rows_total, lats), lambda i, w, s, o: (o[0] + i, 0, 0)),
            ]
            + [whole(x) for x in consts],
            out_specs=block,
        ),
        out_shape=jax.ShapeDtypeStruct(data.shape, BF16),
        compiler_params=pltpu.CompilerParams(vmem_limit_bytes=56 * 2**20),
    )(my_waves, my_starts, first_block, data, legendre, *consts)


def spread_kernel(slots, block, data_ref, spread_ref, out_ref, held):
    step = pl.program_id(0)
    waves = data_ref.shape[0]
    width = data_ref.shape[2] // 2
    span = LANES

    @pl.when(step == 0)
    def _():
        chunk = 16

        @pl.loop(0, waves // chunk)
        def _(i):
            piece = data_ref[pl.ds(i * chunk, chunk)].astype(F32)
            held[pl.ds(pl.multiple_of(i * chunk * slots, 8), chunk * slots), :] = piece.reshape(
                chunk * slots, 2 * width
            )

    turned = [
        held[pl.ds(step * block + s, waves, stride=slots), :].T.astype(BF16) for s in range(block)
    ]
    for b in range(waves // span):
        part = slice(b * span, (b + 1) * span)
        lhs = jnp.concatenate(
            [jnp.concatenate([t[:width, part], t[width:, part]], 1) for t in turned], 0
        )
        got = jnp.dot(lhs, spread_ref[...], preferred_element_type=F32).astype(BF16)
        for s in range(block):
            out_ref[:, s, :, 2 * b * span : 2 * (b + 1) * span] = got[
                s * width : (s + 1) * width
            ].reshape(width // 2, 2, 2 * span)


def spread(data, fields):
    waves, slots, part = data.shape
    block = 4 if slots % 4 == 0 else (2 if slots % 2 == 0 else 1)
    span = LANES
    source = jnp.arange(2 * span, dtype=jnp.int32)
    goal = 2 * (source % span) + source // span
    matrix = (goal[:, None] == source[None, :]).astype(BF16)
    return pl.pallas_call(
        functools.partial(spread_kernel, slots, block),
        grid=(slots // block,),
        in_specs=[
            pl.BlockSpec(data.shape, lambda i: (0, 0, 0)),
            pl.BlockSpec(matrix.shape, lambda i: (0, 0)),
        ],
        out_specs=pl.BlockSpec((fields, block, 2, 2 * waves), lambda i: (0, i, 0, 0)),
        out_shape=jax.ShapeDtypeStruct((fields, slots, 2, 2 * waves), BF16),
        scratch_shapes=[pltpu.VMEM((waves * slots, part), F32)],
        compiler_params=pltpu.CompilerParams(vmem_limit_bytes=56 * 2**20),
    )(data, matrix)


def local(grid, lat_order, wave_order, trim, legendre, modes_in, modes_out, implicit):
    fields, slots = grid.shape[0], grid.shape[1]
    owners, levels = lax.axis_size("wave"), lax.axis_size("lev")
    mine = legendre.shape[0] // levels
    lev = lax.axis_index("lev")
    first = (lax.axis_index("wave") * levels + lev) * mine
    my_waves = lax.dynamic_slice_in_dim(wave_order, first, mine)
    my_starts = LBLK * jnp.sum(
        jnp.where(my_waves[:, None] == jnp.arange(trim.shape[0])[None, :], trim[None, :], 0), 1
    )
    spectra = dft(grid, wave_order)
    sent = lax.all_to_all(spectra, ("wave", "lev"), split_axis=0, concat_axis=0, tiled=True)
    data = sent.reshape(owners, levels, mine, slots, 4 * fields)
    back = spectral(
        data, legendre, (lev * mine)[None], my_waves, my_starts, lat_order, modes_in, modes_out, implicit
    )
    back = back.reshape(spectra.shape)
    back = lax.all_to_all(back, ("wave", "lev"), split_axis=0, concat_axis=0, tiled=True)
    return spread(back, fields)


def solution(mesh):
    in_specs = (
        P(("member", "lev"), "wave", None, None),
        P(),
        P(),
        P(),
        P("wave", None, None),
        P(),
        P(),
        P(),
    )
    out_specs = P(("member", "lev"), "wave", None, None)
    return jax.shard_map(local, mesh=mesh, in_specs=in_specs, out_specs=out_specs, check_vma=False)
```

time: 928 us -> 409 us (0.44); the launches traced: 910 us -> 407 us
  local copies, waits for them, and re-layouts: 386 us -> 48 us
  blocking collectives: 255 us -> 0 us
  waiting for transfers between devices: 82.5 us -> 234 us
  Pallas kernels: 0 us -> 104 us
  matrix products: 97.7 us -> 0 us
  other arithmetic: 82.7 us -> 9.65 us
    all_to_all x3 -> x0, blocking collectives: 255 us -> none  [the longest x1 232 us: local(): lax.all_to_all(result, 'wave', split_axis=1, concat_axis=3, tiled=True)]
    all_to_all x1 -> x2, waiting for transfers between devices: 82.5 us -> 234 us  [the longest x1 142 us: local(): lax.all_to_all(back, ('wave', 'lev'), split_axis=0, concat_axis=0, tiled=...]
    pallas_call x0 -> x3, Pallas kernels: none -> 104 us  [the longest x1 72.9 us: spectral(): pl.pallas_call(functools.partial(spectral_kernel, rows_total), grid_spec=...]
    dot_general x5 -> x0, matrix products: 97.7 us -> none  [the longest x1 29.8 us: inverse(): jnp.einsum('wael,waex->welx', paired, flattened, preferred_element_type=j...]
    all_to_all x5 -> x0, local copies, waits for them, and re-layouts: 77.5 us -> none  [the longest x2 35.2 us: local(): lax.all_to_all(result, 'wave', split_axis=1, concat_axis=3, tiled=True)]
    unnamed x17 -> x16, local copies, waits for them, and re-layouts: 119 us -> 44.5 us
    reshape x4 -> x0, local copies, waits for them, and re-layouts: 57.7 us -> none  [the longest x2 26.2 us: local(): lax.optimization_barrier(spectra).astype(jnp.float32)]
    convert_element_type x5 -> x4, local copies, waits for them, and re-layouts: 47.2 us -> 2 us  [the longest x2 0.96 us: spectral(): mix_out = mix_out.reshape(4 * modes, width).astype(BF16)]
  transfers between devices with their start and end apart: 1 -> 2, of which waited for: 1 -> 2; matrix products, arithmetic and copies ran while one was open for 6% -> 13% of each run, Pallas kernels for 0% -> 0%
where the time goes in v1:
time: 409 us; the launch traced here: 407 us
  waiting for transfers between devices  234 us (57%)
  Pallas kernels  104 us (25%)
  local copies, waits for them, and re-layouts  48 us (12%)
  starting transfers between devices  11.6 us (3%)
  other arithmetic  9.65 us (2%)
    all_to_all x1, waiting for transfers between devices, local(): lax.all_to_all(back, ('wave', 'lev'), split_axis=0, concat_axis=0, tiled=...  142 us
    all_to_all x1, waiting for transfers between devices, local(): lax.all_to_all(spectra, ('wave', 'lev'), split_axis=0, concat_axis=0, til...  91.9 us
    pallas_call x1, Pallas kernels, spectral(): pl.pallas_call(functools.partial(spectral_kernel, rows_total), grid_spec=...  72.9 us
    unnamed x16, local copies, waits for them, and re-layouts  44.5 us
    pallas_call x1, Pallas kernels, dft(): pl.pallas_call(functools.partial(dft_kernel, slots, block), grid=(slots /...  20.1 us
    pallas_call x1, Pallas kernels, spread(): pl.pallas_call(functools.partial(spread_kernel, slots, block), grid=(slot...  10.8 us
  transfers between devices with their start and end apart: 2, of which 2 were waited for; matrix products, arithmetic and copies ran while one was open for 13% of the time, Pallas kernels for 0%

profile of v1, /device:TPU:15, one launch (start us, length us, event | category | flops | bytes accessed | tf_op | source)
XLA Modules:
  0.0 407.3 jit_solution(15673970615525916639)
XLA Ops:
  0.0 3.0 fusion.6
  3.0 0.8 fusion.12
  3.8 0.2 copy.22
  3.9 1.9 sine_multiply_fusion
  5.9 20.1 %shard_map.91 = bf16[640,40,128]{2,1,0:T(8,128)(2,1)} custom-call(bf16[32,40,2,1280]{3,2,1,0:T(2,128)(2,1)} %grid_ref.1, f32[640,10]{1,0:T(8,128)} %get-tuple-element.6.cos_a, f32[640,10]{1,0:T(8,128)} %get-tuple-element.5.sin_a, f32[640,128]{1,0:T(8,128)} %get-tuple-element.8.cos_b, f32[640,128]{1,0:T(8,128)} %get-tuple-element.7.sin_b), custom_call_target="tpu_custom_call" | custom-call | tf_op jit(solution)/shard_map/pallas_call | solution.py:70
  26.0 0.0 copy-start
  26.0 0.0 copy-start.5
  26.0 0.0 copy-start.1
  26.0 6.7 %all-to-all-start = ((bf16[640,40,128]{2,1,0:T(8,128)(2,1)}), bf16[640,40,128]{2,1,0:T(8,128)(2,1)}, u32[]{:S(2)}, u32[]{:S(2)}) async-start(bf16[640,40,128]{2,1,0:T(8,128)(2,1)} %shard_map.91), calls=%async_computation | async-start | bytes 13107200 | tf_op jit(solution)/shard_map/all_to_all | solution.py:228
  32.7 0.8 dynamic_slice.3.wave_ref
  33.5 0.0 copy-start.4
  33.5 0.0 copy-done
  33.5 0.0 copy-done.5
  33.5 0.1 broadcast_multiply_fusion
  33.6 0.2 fusion.10
  33.8 0.2 convert_element_type.40
  34.0 0.8 copy.26.mix_out
  34.8 0.1 copy.23
  34.9 0.0 copy-done.1
  34.9 0.1 copy.24
  35.0 0.2 fusion.9
  35.2 0.9 convert_element_type.37.mix_in
  36.1 0.0 copy-start.6
  36.1 0.0 copy-start.3
  36.1 0.0 copy-start.2
  36.1 44.4 %copy.25.legendre_ref = bf16[80,640,320]{2,1,0:T(8,128)(2,1)} copy(bf16[80,640,320]{1,2,0:T(8,128)(2,1)} %param.13) | data formatting | bytes 65536000 | tf_op args[4]
  80.5 0.0 copy-done.6
  80.5 0.6 broadcast_in_dim_tile.3.implicit_ref
  81.2 0.0 copy-done.4
  81.2 0.0 copy-done.3
  81.2 0.2 select_reduce_fusion
  81.3 0.5 broadcast_multiply_fusion.1.start_ref
  81.9 0.0 copy-done.2
  81.9 0.9 fusion.1
  82.8 1.0 iota_select_fusion.keep_code
  83.8 91.9 %all-to-all-done = bf16[640,40,128]{2,1,0:T(8,128)(2,1)} async-done(((bf16[640,40,128]{2,1,0:T(8,128)(2,1)}), bf16[640,40,128]{2,1,0:T(8,128)(2,1)}, u32[]{:S(2)}, u32[]{:S(2)}) %all-to-all-start) | async-done | bytes 6553632 | tf_op jit(solution)/shard_map/all_to_all | solution.py:228
  175.7 72.9 %shard_map.92 = bf16[8,2,40,40,128]{4,3,2,1,0:T(8,128)(2,1)} custom-call(s32[40]{0:T(128)} %copy-done.4, s32[40]{0:T(128)} %broadcast_multiply_fusion.1.start_ref, s32[1]{0:T(128)} %bitcast.block_ref, bf16[8,2,40,40,128]{4,3,2,1,0:T(8,128)(2,1)} %bitcast.1.data_ref, bf16[80,640,320]{2,1,0:T(8,128)(2,1)} %copy.25.legendre_ref, ...), custom_call_target="tpu_custom_call" | custom-call | tf_op jit(solution)/shard_map/pallas_call | solution.py:147
  248.6 4.9 %all-to-all-start.1 = ((bf16[640,40,128]{2,1,0:T(8,128)(2,1)}), bf16[640,40,128]{2,1,0:T(8,128)(2,1)}, u32[]{:S(2)}, u32[]{:S(2)}) async-start(bf16[640,40,128]{2,1,0:T(8,128)(2,1)} %bitcast.16), calls=%async_computation.1 | async-start | bytes 13107200 | tf_op jit(solution)/shard_map/all_to_all | solution.py:234
  253.5 0.8 fusion.11.spread_ref
  254.3 142.3 %all-to-all-done.1.data_ref = bf16[640,40,128]{2,1,0:T(8,128)(2,1)} async-done(((bf16[640,40,128]{2,1,0:T(8,128)(2,1)}), bf16[640,40,128]{2,1,0:T(8,128)(2,1)}, u32[]{:S(2)}, u32[]{:S(2)}) %all-to-all-start.1) | async-done | bytes 6553632 | tf_op jit(solution)/shard_map/all_to_all | solution.py:234
  396.5 10.8 %shard_map.93 = bf16[32,40,2,1280]{3,2,1,0:T(2,128)(2,1)} custom-call(bf16[640,40,128]{2,1,0:T(8,128)(2,1)} %all-to-all-done.1.data_ref, bf16[256,256]{1,0:T(8,128)(2,1)} %fusion.11.spread_ref), custom_call_target="tpu_custom_call" | custom-call | tf_op jit(solution)/shard_map/pallas_call | solution.py:203
  (8 shorter events, 0.0 us)
Async XLA Ops:
  26.0 7.5 %copy-start = (bf16[64,64]{1,0:T(8,128)(2,1)S(1)}, bf16[64,64]{1,0:T(8,128)(2,1)}, u32[]{:S(2)}) copy-start(bf16[64,64]{1,0:T(8,128)(2,1)} %param.15) | copy-start | bytes 24580
  26.0 7.5 %copy-start.5 = (f32[2,2]{1,0:T(2,128)S(1)}, f32[2,2]{1,0:T(2,128)}, u32[]{:S(2)}) copy-start(f32[2,2]{1,0:T(2,128)} %constant.95.clone) | copy-start | bytes 52
  26.0 8.9 %copy-start.1 = (bf16[64,64]{1,0:T(8,128)(2,1)S(1)}, bf16[64,64]{1,0:T(8,128)(2,1)}, u32[]{:S(2)}) copy-start(bf16[64,64]{1,0:T(8,128)(2,1)} %param.14) | copy-start | bytes 24580
  26.0 149.8 %all-to-all-start = ((bf16[640,40,128]{2,1,0:T(8,128)(2,1)}), bf16[640,40,128]{2,1,0:T(8,128)(2,1)}, u32[]{:S(2)}, u32[]{:S(2)}) async-start(bf16[640,40,128]{2,1,0:T(8,128)(2,1)} %shard_map.91), calls=%async_computation | async-start | bytes 13107200 | tf_op jit(solution)/shard_map/all_to_all | solution.py:228
  33.5 47.7 %copy-start.4 = (s32[40]{0:T(128)}, s32[40]{0:T(128)S(1)}, u32[]{:S(2)}) copy-start(s32[40]{0:T(128)S(1)} %dynamic_slice.3.wave_ref) | copy-start | bytes 484
  36.1 44.4 %copy-start.6 = (f32[64]{0:T(128)S(1)}, f32[64]{0:T(128)}, u32[]{:S(2)}) copy-start(f32[64]{0:T(128)} %param.16) | copy-start | bytes 772
  36.1 45.0 %copy-start.3 = (s32[640]{0:T(1024)S(1)}, s32[640]{0:T(1024)}, u32[]{:S(2)}) copy-start(s32[640]{0:T(1024)} %param.12) | copy-start | bytes 7684
  36.1 45.8 %copy-start.2 = (s32[320]{0:T(512)S(1)}, s32[320]{0:T(512)}, u32[]{:S(2)}) copy-start(s32[320]{0:T(512)} %param.10) | copy-start | bytes 3844
  248.6 147.9 %all-to-all-start.1 = ((bf16[640,40,128]{2,1,0:T(8,128)(2,1)}), bf16[640,40,128]{2,1,0:T(8,128)(2,1)}, u32[]{:S(2)}, u32[]{:S(2)}) async-start(bf16[640,40,128]{2,1,0:T(8,128)(2,1)} %bitcast.16), calls=%async_computation.1 | async-start | bytes 13107200 | tf_op jit(solution)/shard_map/all_to_all | solution.py:234

commit v2 on v1

--- a/solution.py
+++ b/solution.py
@@ -10,6 +10,7 @@
 
 LBLK = 64
 LANES = 128
+CHUNKS = 2
 F32 = jnp.float32
 BF16 = jnp.bfloat16
 
@@ -79,6 +80,11 @@
             pltpu.VMEM((waves * slots, 4 * fields), F32),
         ],
         compiler_params=pltpu.CompilerParams(vmem_limit_bytes=56 * 2**20),
+        cost_estimate=pl.CostEstimate(
+            flops=4 * waves * lon_count * fields * slots * 2,
+            bytes_accessed=4 * grid.size,
+            transcendentals=0,
+        ),
     )(grid, *tables)
 
 
@@ -104,14 +110,14 @@
     )
     sym = jnp.where(lat_ok, sym, 0.0).astype(BF16)
     basis = legendre_ref[0]
-    y = jnp.dot(basis, sym, preferred_element_type=F32)
+    y = lax.dot_general(basis, sym, (((0,), (0,)), ((), ())), preferred_element_type=F32)
     y = jnp.where(keep_code[...] < rows_total - m, y, 0.0).astype(BF16)
     modal = jnp.dot(y, mix_in[...], preferred_element_type=F32)
     degree = (m + lax.broadcasted_iota(jnp.int32, (rows_total, 1), 0)).astype(F32)
     factor = degree * (degree + 1.0) / float(rows_total * (rows_total - 1))
     scaled = (modal / (1.0 + factor * implicit_ref[...])).astype(BF16)
     solved = jnp.dot(scaled, mix_out[...], preferred_element_type=F32).astype(BF16)
-    o = lax.dot_general(basis, solved, (((0,), (0,)), ((), ())), preferred_element_type=F32)
+    o = jnp.dot(basis, solved, preferred_element_type=F32)
     o = jnp.where(lat_ok, o, 0.0).astype(BF16)
     o = jnp.dot(to_slot[...], o, preferred_element_type=F32).astype(BF16)
     for v in range(levels):
@@ -122,7 +128,7 @@
     data, legendre, first_block, my_waves, my_starts, lat_order, modes_in, modes_out, implicit
 ):
     owners, levels, mine, slots, part = data.shape
-    rows_total, lats = legendre.shape[1], legendre.shape[2]
+    lats, rows_total = legendre.shape[1], legendre.shape[2]
     fields = part // 4
     width = levels * part
     order = jnp.arange(lats, dtype=jnp.int32)
@@ -151,32 +157,40 @@
             grid=(mine,),
             in_specs=[
                 block,
-                pl.BlockSpec((1, rows_total, lats), lambda i, w, s, o: (o[0] + i, 0, 0)),
+                pl.BlockSpec((1, lats, rows_total), lambda i, w, s, o: (o[0] + i, 0, 0)),
             ]
             + [whole(x) for x in consts],
             out_specs=block,
         ),
         out_shape=jax.ShapeDtypeStruct(data.shape, BF16),
         compiler_params=pltpu.CompilerParams(vmem_limit_bytes=56 * 2**20),
+        cost_estimate=pl.CostEstimate(
+            flops=4 * mine * width * (lats + rows_total) * (lats + width),
+            bytes_accessed=2 * mine * rows_total * lats + 4 * data.size,
+            transcendentals=0,
+        ),
     )(my_waves, my_starts, first_block, data, legendre, *consts)
 
 
-def spread_kernel(slots, block, data_ref, spread_ref, out_ref, held):
+def spread_kernel(slots, block, parts, mine, *refs):
+    data_refs, (spread_ref, out_ref, held) = refs[:parts], refs[parts:]
     step = pl.program_id(0)
-    waves = data_ref.shape[0]
-    width = data_ref.shape[2] // 2
+    waves = held.shape[0] // slots
+    width = held.shape[1] // 2
     span = LANES
+    share = mine // parts
 
     @pl.when(step == 0)
     def _():
-        chunk = 16
-
-        @pl.loop(0, waves // chunk)
-        def _(i):
-            piece = data_ref[pl.ds(i * chunk, chunk)].astype(F32)
-            held[pl.ds(pl.multiple_of(i * chunk * slots, 8), chunk * slots), :] = piece.reshape(
-                chunk * slots, 2 * width
-            )
+        for c in range(parts):
+
+            @pl.loop(0, waves // mine)
+            def _(d):
+                piece = data_refs[c][pl.ds(d * share, share)].astype(F32)
+                start = (d * mine + c * share) * slots
+                if share * slots % 8 == 0:
+                    start = pl.multiple_of(start, 8)
+                held[pl.ds(start, share * slots), :] = piece.reshape(share * slots, 2 * width)
 
     turned = [
         held[pl.ds(step * block + s, waves, stride=slots), :].T.astype(BF16) for s in range(block)
@@ -193,25 +207,28 @@
             ].reshape(width // 2, 2, 2 * span)
 
 
-def spread(data, fields):
-    waves, slots, part = data.shape
+def spread(datas, fields, mine):
+    slots, part = datas[0].shape[1:]
+    waves = sum(d.shape[0] for d in datas)
     block = 4 if slots % 4 == 0 else (2 if slots % 2 == 0 else 1)
     span = LANES
     source = jnp.arange(2 * span, dtype=jnp.int32)
     goal = 2 * (source % span) + source // span
     matrix = (goal[:, None] == source[None, :]).astype(BF16)
     return pl.pallas_call(
-        functools.partial(spread_kernel, slots, block),
+        functools.partial(spread_kernel, slots, block, len(datas), mine),
         grid=(slots // block,),
-        in_specs=[
-            pl.BlockSpec(data.shape, lambda i: (0, 0, 0)),
-            pl.BlockSpec(matrix.shape, lambda i: (0, 0)),
-        ],
+        in_specs=[pl.BlockSpec(d.shape, lambda i: (0, 0, 0)) for d in datas]
+        + [pl.BlockSpec(matrix.shape, lambda i: (0, 0))],
         out_specs=pl.BlockSpec((fields, block, 2, 2 * waves), lambda i: (0, i, 0, 0)),
         out_shape=jax.ShapeDtypeStruct((fields, slots, 2, 2 * waves), BF16),
         scratch_shapes=[pltpu.VMEM((waves * slots, part), F32)],
         compiler_params=pltpu.CompilerParams(vmem_limit_bytes=56 * 2**20),
-    )(data, matrix)
+    )(*datas, matrix)
+
+
+def exchange(x):
+    return lax.all_to_all(x, ("wave", "lev"), split_axis=0, concat_axis=0, tiled=True)
 
 
 def local(grid, lat_order, wave_order, trim, legendre, modes_in, modes_out, implicit):
@@ -224,15 +241,24 @@
     my_starts = LBLK * jnp.sum(
         jnp.where(my_waves[:, None] == jnp.arange(trim.shape[0])[None, :], trim[None, :], 0), 1
     )
-    spectra = dft(grid, wave_order)
-    sent = lax.all_to_all(spectra, ("wave", "lev"), split_axis=0, concat_axis=0, tiled=True)
-    data = sent.reshape(owners, levels, mine, slots, 4 * fields)
-    back = spectral(
-        data, legendre, (lev * mine)[None], my_waves, my_starts, lat_order, modes_in, modes_out, implicit
-    )
-    back = back.reshape(spectra.shape)
-    back = lax.all_to_all(back, ("wave", "lev"), split_axis=0, concat_axis=0, tiled=True)
-    return spread(back, fields)
+    chunks = CHUNKS if mine % CHUNKS == 0 else 1
+    share = mine // chunks
+    orders = wave_order.reshape(owners * levels, chunks, share)
+    turned = legendre.transpose(0, 2, 1)
+    received = []
+    for c in range(chunks):
+        spectra = dft(grid, orders[:, c].reshape(-1))
+        received.append(exchange(spectra))
+    returned = []
+    for c in range(chunks):
+        data = received[c].reshape(owners, levels, share, slots, 4 * fields)
+        mid = slice(c * share, (c + 1) * share)
+        back = spectral(
+            data, turned, (lev * mine + c * share)[None], my_waves[mid], my_starts[mid],
+            lat_order, modes_in, modes_out, implicit,
+        )
+        returned.append(exchange(back.reshape(received[c].shape)))
+    return spread(returned, fields, mine)
 
 
 def solution(mesh):

time: 409 us -> 345 us (0.84)
  waiting for transfers between devices: 234 us -> 191 us
  local copies, waits for them, and re-layouts: 48 us -> 8.78 us
  Pallas kernels: 104 us -> 114 us
  starting transfers between devices: 11.6 us -> 21.3 us
    all_to_all x2 -> x4, waiting for transfers between devices: 234 us -> 191 us  [exchange(): lax.all_to_all(x, ('wave', 'lev'), split_axis=0, concat_axis=0, tiled=True)]
    unnamed x16 -> x17, local copies, waits for them, and re-layouts: 44.5 us -> 3.56 us
    all_to_all x2 -> x4, starting transfers between devices: 11.6 us -> 21.3 us  [exchange(): lax.all_to_all(x, ('wave', 'lev'), split_axis=0, concat_axis=0, tiled=True)]
    pallas_call x1 -> x2, Pallas kernels: 20.1 us -> 27.3 us  [dft(): pl.pallas_call(functools.partial(dft_kernel, slots, block), grid=(slots /...]
    pallas_call x1 -> x2, Pallas kernels: 72.9 us -> 76 us  [spectral(): pl.pallas_call(functools.partial(spectral_kernel, rows_total), grid_spec=...]
  transfers between devices with their start and end apart: 2 -> 4, of which waited for: 2 -> 4; matrix products, arithmetic and copies ran while one was open for 13% -> 3% of each run, Pallas kernels for 0% -> 26%
where the time goes in v2:
time: 345 us; the launch traced here: 344 us
  waiting for transfers between devices  191 us (55%)
  Pallas kernels  114 us (33%)
  starting transfers between devices  21.3 us (6%)
  other arithmetic  9.17 us (3%)
  local copies, waits for them, and re-layouts  8.78 us (3%)
    all_to_all x4, waiting for transfers between devices, exchange(): lax.all_to_all(x, ('wave', 'lev'), split_axis=0, concat_axis=0, tiled=True)  191 us
    pallas_call x2, Pallas kernels, spectral(): pl.pallas_call(functools.partial(spectral_kernel, rows_total), grid_spec=...  76 us
    pallas_call x2, Pallas kernels, dft(): pl.pallas_call(functools.partial(dft_kernel, slots, block), grid=(slots /...  27.3 us
    all_to_all x4, starting transfers between devices, exchange(): lax.all_to_all(x, ('wave', 'lev'), split_axis=0, concat_axis=0, tiled=True)  21.3 us
    pallas_call x1, Pallas kernels, spread(): pl.pallas_call(functools.partial(spread_kernel, slots, block, len(datas),...  10.8 us
  transfers between devices with their start and end apart: 4, of which 4 were waited for; matrix products, arithmetic and copies ran while one was open for 3% of the time, Pallas kernels for 26%

profile of v2, /device:TPU:15, one launch (start us, length us, event | category | flops | bytes accessed | tf_op | source)
XLA Modules:
  0.0 344.2 jit_solution(2967363850835297584)
XLA Ops:
  0.0 0.8 reshape.96
  0.9 0.1 mul.131
  0.9 0.1 mul.119
  1.0 1.5 fusion.11
  2.5 0.1 fusion.20
  2.6 0.1 copy.26
  2.7 1.3 sine_multiply_fusion
  4.1 13.7 %shard_map.102 = bf16[320,40,128]{2,1,0:T(8,128)(2,1)} custom-call(bf16[32,40,2,1280]{3,2,1,0:T(2,128)(2,1)} %grid_ref.3, f32[320,10]{1,0:T(8,128)} %get-tuple-element.8.cos_a, f32[320,10]{1,0:T(8,128)} %get-tuple-element.7.sin_a, f32[320,128]{1,0:T(8,128)} %get-tuple-element.12.cos_b, f32[320,128]{1,0:T(8,128)} %get-tuple-element.11.sin_b), custom_call_target="tpu_custom_call" | custom-call | flops 4194304000 | bytes 13107200 | tf_op jit(solution)/shard_map/pallas_call | solution.py:71
  17.7 6.6 %all-to-all-start.2 = ((bf16[320,40,128]{2,1,0:T(8,128)(2,1)}), bf16[320,40,128]{2,1,0:T(8,128)(2,1)S(1)}, u32[]{:S(2)}, u32[]{:S(2)}) async-start(bf16[320,40,128]{2,1,0:T(8,128)(2,1)} %shard_map.102), calls=%async_computation.2 | async-start | bytes 6553600 | tf_op jit(solution)/shard_map/all_to_all | solution.py:231
  24.3 0.1 copy.22
  24.4 1.5 fusion.15
  25.9 1.3 sine_multiply_fusion.1
  27.2 13.7 %shard_map.100 = bf16[320,40,128]{2,1,0:T(8,128)(2,1)} custom-call(bf16[32,40,2,1280]{3,2,1,0:T(2,128)(2,1)} %grid_ref.3, f32[320,10]{1,0:T(8,128)} %get-tuple-element.10.cos_a, f32[320,10]{1,0:T(8,128)} %get-tuple-element.9.sin_a, f32[320,128]{1,0:T(8,128)} %get-tuple-element.16.cos_b, f32[320,128]{1,0:T(8,128)} %get-tuple-element.15.sin_b), custom_call_target="tpu_custom_call" | custom-call | flops 4194304000 | bytes 13107200 | tf_op jit(solution)/shard_map/pallas_call | solution.py:71
  40.9 0.0 copy-start.7
  40.9 0.0 copy-start.6
  40.9 0.0 copy-start.3
  40.9 0.0 copy-start.2
  40.9 0.0 copy-start.5
  40.9 0.0 copy-start.4
  40.9 56.0 %all-to-all-done.2 = bf16[320,40,128]{2,1,0:T(8,128)(2,1)S(1)} async-done(((bf16[320,40,128]{2,1,0:T(8,128)(2,1)}), bf16[320,40,128]{2,1,0:T(8,128)(2,1)S(1)}, u32[]{:S(2)}, u32[]{:S(2)}) %all-to-all-start.2) | async-done | bytes 3276832 | tf_op jit(solution)/shard_map/all_to_all | solution.py:231
  97.0 0.0 copy-start.1
  97.0 1.7 copy-done.1
  98.7 4.9 %all-to-all-start = ((bf16[320,40,128]{2,1,0:T(8,128)(2,1)}), bf16[320,40,128]{2,1,0:T(8,128)(2,1)}, u32[]{:S(2)}, u32[]{:S(2)}) async-start(bf16[320,40,128]{2,1,0:T(8,128)(2,1)} %shard_map.100), calls=%async_computation | async-start | bytes 6553600 | tf_op jit(solution)/shard_map/all_to_all | solution.py:231
  103.6 0.8 dynamic_slice.3
  104.3 0.0 copy-done.7
  104.4 0.6 broadcast_in_dim_tile.4.implicit_ref
  105.0 0.0 copy-done.6
  105.0 0.1 broadcast_multiply_fusion
  105.0 0.1 copy.23
  105.2 0.0 copy-done.3
  105.2 0.1 copy.24
  105.3 0.0 copy-done.2
  105.3 0.2 fusion.3
  105.5 0.2 convert_element_type.58
  105.7 0.8 copy.25.mix_out
  106.5 0.2 fusion.2
  106.7 0.9 convert_element_type.55.mix_in
  107.6 0.0 copy-done.5
  107.6 0.2 select_reduce_fusion
  107.8 0.7 fusion.34
  108.5 0.0 copy-done.4
  108.5 0.9 fusion.1
  109.4 1.0 iota_select_fusion.keep_code
  110.4 38.0 %shard_map.103 = bf16[8,2,20,40,128]{4,3,2,1,0:T(8,128)(2,1)} custom-call(s32[20]{0:T(128)} %get-tuple-element.26.wave_ref, s32[20]{0:T(128)} %get-tuple-element.21.start_ref, s32[1]{0:T(128)} %bitcast.10.block_ref, bf16[8,2,20,40,128]{4,3,2,1,0:T(8,128)(2,1)} %bitcast.20, bf16[80,320,640]{2,1,0:T(8,128)(2,1)} %bitcast.25, ...), custom_call_target="tpu_custom_call" | custom-call | flops 11324620800 | bytes 14745600 | tf_op jit(solution)/shard_map/pallas_call | solution.py:153
  148.4 28.0 %all-to-all-done = bf16[320,40,128]{2,1,0:T(8,128)(2,1)} async-done(((bf16[320,40,128]{2,1,0:T(8,128)(2,1)}), bf16[320,40,128]{2,1,0:T(8,128)(2,1)}, u32[]{:S(2)}, u32[]{:S(2)}) %all-to-all-start) | async-done | bytes 3276832 | tf_op jit(solution)/shard_map/all_to_all | solution.py:231
  176.4 4.9 %all-to-all-start.3 = ((bf16[320,40,128]{2,1,0:T(8,128)(2,1)}), bf16[320,40,128]{2,1,0:T(8,128)(2,1)S(1)}, u32[]{:S(2)}, u32[]{:S(2)}) async-start(bf16[320,40,128]{2,1,0:T(8,128)(2,1)} %bitcast.21), calls=%async_computation.3 | async-start | bytes 6553600 | tf_op jit(solution)/shard_map/all_to_all | solution.py:231
  181.3 38.0 %shard_map.101 = bf16[8,2,20,40,128]{4,3,2,1,0:T(8,128)(2,1)} custom-call(s32[20]{0:T(128)} %get-tuple-element.25.wave_ref, s32[20]{0:T(128)} %get-tuple-element.22.start_ref, s32[1]{0:T(128)} %bitcast.block_ref, bf16[8,2,20,40,128]{4,3,2,1,0:T(8,128)(2,1)} %bitcast.1.data_ref, bf16[80,320,640]{2,1,0:T(8,128)(2,1)} %bitcast.26, ...), custom_call_target="tpu_custom_call" | custom-call | flops 11324620800 | bytes 14745600 | tf_op jit(solution)/shard_map/pallas_call | solution.py:153
  219.3 34.7 %all-to-all-done.3.refs_1_ = bf16[320,40,128]{2,1,0:T(8,128)(2,1)S(1)} async-done(((bf16[320,40,128]{2,1,0:T(8,128)(2,1)}), bf16[320,40,128]{2,1,0:T(8,128)(2,1)S(1)}, u32[]{:S(2)}, u32[]{:S(2)}) %all-to-all-start.3) | async-done | bytes 3276832 | tf_op jit(solution)/shard_map/all_to_all | solution.py:231
  254.0 0.0 copy-start
  254.0 1.7 copy-done
  255.7 4.9 %all-to-all-start.1 = ((bf16[320,40,128]{2,1,0:T(8,128)(2,1)}), bf16[320,40,128]{2,1,0:T(8,128)(2,1)}, u32[]{:S(2)}, u32[]{:S(2)}) async-start(bf16[320,40,128]{2,1,0:T(8,128)(2,1)} %bitcast.22), calls=%async_computation.1 | async-start | bytes 6553600 | tf_op jit(solution)/shard_map/all_to_all | solution.py:231
  260.6 0.8 fusion.4.refs_2_
  261.4 72.0 %all-to-all-done.1.refs_0_ = bf16[320,40,128]{2,1,0:T(8,128)(2,1)} async-done(((bf16[320,40,128]{2,1,0:T(8,128)(2,1)}), bf16[320,40,128]{2,1,0:T(8,128)(2,1)}, u32[]{:S(2)}, u32[]{:S(2)}) %all-to-all-start.1) | async-done | bytes 3276832 | tf_op jit(solution)/shard_map/all_to_all | solution.py:231
  333.4 10.8 %shard_map.104 = bf16[32,40,2,1280]{3,2,1,0:T(2,128)(2,1)} custom-call(bf16[320,40,128]{2,1,0:T(8,128)(2,1)} %all-to-all-done.1.refs_0_, bf16[320,40,128]{2,1,0:T(8,128)(2,1)} %copy-done, bf16[256,256]{1,0:T(8,128)(2,1)} %fusion.4.refs_2_), custom_call_target="tpu_custom_call" | custom-call | tf_op jit(solution)/shard_map/pallas_call | solution.py:218
  (10 shorter events, 0.1 us)
Async XLA Ops:
  17.7 79.3 %all-to-all-start.2 = ((bf16[320,40,128]{2,1,0:T(8,128)(2,1)}), bf16[320,40,128]{2,1,0:T(8,128)(2,1)S(1)}, u32[]{:S(2)}, u32[]{:S(2)}) async-start(bf16[320,40,128]{2,1,0:T(8,128)(2,1)} %shard_map.102), calls=%async_computation.2 | async-start | bytes 6553600 | tf_op jit(solution)/shard_map/all_to_all | solution.py:231
  40.9 63.5 %copy-start.7 = (f32[64]{0:T(128)S(1)}, f32[64]{0:T(128)}, u32[]{:S(2)}) copy-start(f32[64]{0:T(128)} %param.17) | copy-start | bytes 772
  40.9 64.1 %copy-start.6 = (f32[2,2]{1,0:T(2,128)S(1)}, f32[2,2]{1,0:T(2,128)}, u32[]{:S(2)}) copy-start(f32[2,2]{1,0:T(2,128)} %constant.109.clone) | copy-start | bytes 52
  40.9 64.3 %copy-start.3 = (bf16[64,64]{1,0:T(8,128)(2,1)S(1)}, bf16[64,64]{1,0:T(8,128)(2,1)}, u32[]{:S(2)}) copy-start(bf16[64,64]{1,0:T(8,128)(2,1)} %param.15) | copy-start | bytes 24580
  40.9 64.4 %copy-start.2 = (bf16[64,64]{1,0:T(8,128)(2,1)S(1)}, bf16[64,64]{1,0:T(8,128)(2,1)}, u32[]{:S(2)}) copy-start(bf16[64,64]{1,0:T(8,128)(2,1)} %param.16) | copy-start | bytes 24580
  40.9 66.7 %copy-start.5 = (s32[640]{0:T(1024)S(1)}, s32[640]{0:T(1024)}, u32[]{:S(2)}) copy-start(s32[640]{0:T(1024)} %param.13) | copy-start | bytes 7684
  40.9 67.6 %copy-start.4 = (s32[320]{0:T(512)S(1)}, s32[320]{0:T(512)}, u32[]{:S(2)}) copy-start(s32[320]{0:T(512)} %param.11) | copy-start | bytes 3844
  97.0 1.7 copy-start.1
  98.7 77.7 %all-to-all-start = ((bf16[320,40,128]{2,1,0:T(8,128)(2,1)}), bf16[320,40,128]{2,1,0:T(8,128)(2,1)}, u32[]{:S(2)}, u32[]{:S(2)}) async-start(bf16[320,40,128]{2,1,0:T(8,128)(2,1)} %shard_map.100), calls=%async_computation | async-start | bytes 6553600 | tf_op jit(solution)/shard_map/all_to_all | solution.py:231
  176.4 77.6 %all-to-all-start.3 = ((bf16[320,40,128]{2,1,0:T(8,128)(2,1)}), bf16[320,40,128]{2,1,0:T(8,128)(2,1)S(1)}, u32[]{:S(2)}, u32[]{:S(2)}) async-start(bf16[320,40,128]{2,1,0:T(8,128)(2,1)} %bitcast.21), calls=%async_computation.3 | async-start | bytes 6553600 | tf_op jit(solution)/shard_map/all_to_all | solution.py:231
  254.0 1.7 copy-start
  255.7 77.7 %all-to-all-start.1 = ((bf16[320,40,128]{2,1,0:T(8,128)(2,1)}), bf16[320,40,128]{2,1,0:T(8,128)(2,1)}, u32[]{:S(2)}, u32[]{:S(2)}) async-start(bf16[320,40,128]{2,1,0:T(8,128)(2,1)} %bitcast.22), calls=%async_computation.1 | async-start | bytes 6553600 | tf_op jit(solution)/shard_map/all_to_all | solution.py:231
